TPU v7x, 128 devices: a whole 4x4x4 slice. The times are simulated.
128 devices in a mesh: section: 2 (over core), block: 64 (over x, z, y).
Axes of the slice: x: 4, y: 4, z: 4, core: 2. Of those that a mesh axis runs over, the one named last changes fastest.
Arguments:
- env: float32 [2, 256, 512, 512], P('section', 'block'), may hold values from -6 to 6
- site: float32 [2, 8192, 2, 512], P('section', 'block'), may hold values from -0.25 to 0.25
- sector_tiles: int32 [16], replicated, may hold values from 1 to 16, 128 in all
- mpo_mask: int32 [2, 16, 16], P('section'), may hold values 0 or 1
- mpo_coef: float32 [2, 2, 16, 16], P('section'), may hold values from -1.5 to 1.5
- psi: float32 [2, 8192, 512], P('section', 'block'), may hold values from -0.03125 to 0.03125
- center_coef: float32 [2, 16], P('section'), may hold values from -1.5 to 1.5
Outputs:
- new_env: float32 [2, 256, 512, 512], P('section', 'block')
- hpsi: float32 [2, 8192, 512], P('section', 'block')
All inputs are finite; a program needn't handle non-finite values. No bound on the sum of `mpo_mask` on one device may be relied on, other than what follows from the above.
Results may differ from a plain program's by a relative error of at most 0.0003.
Values sent between devices are 32-bit elements; how exact they have to be, the bound alone decides.
A program may use at most 192 MiB of HBM per device.

v0:
```python
import jax
import jax.numpy as jnp
from jax import lax
from jax.sharding import PartitionSpec as P

TROW = 32


HIGH = lax.Precision.HIGHEST


def swapped(block, axis, distance):
    count = lax.axis_size(axis)
    route = []
    for low in range(count):
        high = low | 1 << distance
        if high != low and high < count:
            route += [(low, high), (high, low)]
    return lax.ppermute(block, axis, route)


def from_behind(value, axis, steps):
    count = lax.axis_size(axis)
    first, last = (max(0, -steps), min(count, count - steps))
    return lax.ppermute(value, axis, [(source, source + steps) for source in range(first, last)])


def ordered(is_upper, mine, theirs, axis_dim):
    return jnp.where(
        is_upper,
        jnp.concatenate([theirs, mine], axis=axis_dim),
        jnp.concatenate([mine, theirs], axis=axis_dim),
    )


def sandwich(masked, blocks):
    inner = jnp.einsum("wij,jk->wik", blocks, masked, precision=HIGH)
    return jnp.einsum("ji,wjk->wik", masked, inner, precision=HIGH)


def local(env, site, sector_tiles, mpo_mask, mpo_coef, psi, center_coef):
    nsector = sector_tiles.shape[0]
    group = lax.axis_size("block") // nsector
    levels = group.bit_length() - 1
    device = lax.axis_index("block")
    sector = device // group
    member = device % group
    section = lax.axis_index("section")
    width_local = env.shape[1]
    extent = env.shape[2]
    labels = jnp.arange(nsector, dtype=jnp.int32)
    counts = sector_tiles * TROW
    size_here = jnp.sum(jnp.where(labels == sector, counts, 0))
    size_next = jnp.sum(jnp.where(labels == sector + 1, counts, 0))
    span = jnp.arange(extent, dtype=jnp.int32)
    rows_now = site[0]
    wave_now = psi[0]
    for segment in range(levels):
        other_rows, other_wave = swapped((rows_now, wave_now), "block", segment)
        is_upper = member // 2**segment % 2 == 1
        rows_now = ordered(is_upper, rows_now, other_rows, 0)
        wave_now = ordered(is_upper, wave_now, other_wave, 0)
    row_keep = (span < size_here).astype(jnp.float32)
    masks = []
    for spin in range(2):
        limit = size_here if spin == 0 else size_next
        col_keep = (span < limit).astype(jnp.float32)
        masks.append(rows_now[:, spin, :] * row_keep[:, None] * col_keep[None, :])
    blocks = env[0]
    mixing = mpo_coef[0] * mpo_mask[0].astype(jnp.float32)
    collected = jnp.stack([sandwich(masks[0], blocks), sandwich(masks[1], blocks)])
    for segment in range(levels):
        other_terms = swapped(collected, "block", segment)
        is_upper = member // 2**segment % 2 == 1
        collected = ordered(is_upper, collected, other_terms, 1)
    own_cols = lax.dynamic_slice_in_dim(mixing, member * width_local, width_local, 2)
    reduced = jnp.einsum("xwv,xwij->xvij", own_cols, collected, precision=HIGH)
    arrived = from_behind(reduced[1], "block", group)
    fresh = reduced[0] + arrived
    partner = swapped(fresh, "section", 0)
    left_env = jnp.where(section == 0, fresh, partner)
    right_env = jnp.where(section == 0, partner, fresh)
    first = jnp.einsum("wij,jk->wik", left_env, wave_now, precision=HIGH)
    second = jnp.einsum("wij,wjk->wik", first, right_env, precision=HIGH)
    weights = lax.dynamic_slice_in_dim(center_coef[0], member * width_local, width_local, 0)
    summed = jnp.einsum("w,wik->ik", weights, second, precision=HIGH)
    for segment in reversed(range(levels)):
        half_rows = summed.shape[0] // 2
        lower_part = summed[:half_rows]
        upper_part = summed[half_rows:]
        is_upper = member // 2**segment % 2 == 1
        keeping = jnp.where(is_upper, upper_part, lower_part)
        sending = jnp.where(is_upper, lower_part, upper_part)
        summed = keeping + swapped(sending, "block", segment)
    return (fresh[None], summed[None])


def solution(mesh):
    placed = (
        P("section", "block", None, None),
        P("section", "block", None, None),
        P(),
        P("section", None, None),
        P("section", None, None, None),
        P("section", "block", None),
        P("section", None),
    )
    return jax.shard_map(
        local,
        mesh=mesh,
        in_specs=placed,
        out_specs=(P("section", "block", None, None), P("section", "block", None)),
        check_vma=False,
    )
```

profile of v0, /device:TPU:6, one launch (start us, length us, event | category | flops | bytes accessed | tf_op | source)
XLA Modules:
  0.0 904.0 jit_solution(12479706672568147220)
XLA Ops:
  0.6 0.0 copy-start
  0.6 1.7 collective-permute-start
  2.3 12.3 %collective-permute-done = f32[128,2,512]{2,1,0:T(2,128)S(1)} collective-permute-done((f32[128,2,512]{2,1,0:T(2,128)}, f32[128,2,512]{2,1,0:T(2,128)S(1)}, u32[]{:S(2)}, u32[]{:S(2)}) %collective-permute-start) | collective-permute-done | bytes 524320 | tf_op jit(solution)/shard_map/ppermute | solution.py:19
  14.6 2.3 maximum_select_fusion.3
  16.9 3.3 collective-permute-start.1
  20.2 1.3 fusion.62
  21.4 1.3 fusion.57
  22.8 0.0 copy-start.1
  22.8 19.7 %collective-permute-done.1 = f32[256,2,512]{2,1,0:T(2,128)S(1)} collective-permute-done((f32[256,2,512]{2,1,0:T(2,128)S(1)}, f32[256,2,512]{2,1,0:T(2,128)S(1)}, u32[]{:S(2)}, u32[]{:S(2)}) %collective-permute-start.1) | collective-permute-done | bytes 1048608 | tf_op jit(solution)/shard_map/ppermute | solution.py:19
  42.5 1.8 maximum_select_fusion.2
  44.3 1.6 fusion.65
  46.0 13.5 %fusion.7 = f32[512,4,512]{2,0,1:T(8,128)S(1)} fusion(f32[1,4,512,512]{3,2,1,0:T(8,128)S(1)} %copy-done.1, f32[512,1,512]{2,1,0:T(1,128)S(1)} %get-tuple-element.8, f32[512]{0:T(512)S(1)} %get-tuple-element.10), kind=kOutput, calls=%fused_computation.12 | convolution fusion | flops 6442975232 | bytes 9439232 | tf_op jit(solution)/shard_map/wij,jk->wik/dot_general | solution.py:37
  59.5 7.0 fusion.15
  66.5 13.8 %fusion.5 = f32[512,4,512]{2,0,1:T(8,128)S(1)} fusion(f32[1,4,512,512]{3,2,1,0:T(8,128)S(1)} %copy-done.1, f32[512,1,512]{2,1,0:T(1,128)S(1)} %get-tuple-element.9, f32[512]{0:T(512)S(1)} %get-tuple-element.11, f32[512]{0:T(512)S(1)} %get-tuple-element.10), kind=kOutput, calls=%fused_computation.10 | convolution fusion | flops 6442975232 | bytes 9441280 | tf_op jit(solution)/shard_map/wij,jk->wik/dot_general | solution.py:37
  80.3 7.2 fusion.18
  87.5 4.3 pad_maximum_fusion
  91.8 1.6 collective-permute-start.2
  93.4 179.0 %collective-permute-done.2 = f32[2,4,512,512]{2,3,1,0:T(8,128)S(1)} collective-permute-done((f32[2,4,512,512]{2,3,1,0:T(8,128)}, f32[2,4,512,512]{2,3,1,0:T(8,128)S(1)}, u32[]{:S(2)}, u32[]{:S(2)}) %collective-permute-start.2) | collective-permute-done | bytes 8388640 | tf_op jit(solution)/shard_map/ppermute | solution.py:19
  272.4 7.7 maximum_select_fusion.1
  280.1 3.2 collective-permute-start.3
  283.3 0.1 copy.10
  283.4 0.1 copy.9
  283.5 357.7 %collective-permute-done.3 = f32[2,8,512,512]{2,3,1,0:T(8,128)} collective-permute-done((f32[2,8,512,512]{2,3,1,0:T(8,128)}, f32[2,8,512,512]{2,3,1,0:T(8,128)}, u32[]{:S(2)}, u32[]{:S(2)}) %collective-permute-start.3) | collective-permute-done | bytes 16777248 | tf_op jit(solution)/shard_map/ppermute | solution.py:19
  641.2 32.5 %maximum_select_fusion = f32[2,16,512,512]{2,3,1,0:T(8,128)} fusion(f32[2,8,512,512]{2,3,1,0:T(8,128)} %maximum_select_fusion.1, f32[2,8,512,512]{2,3,1,0:T(8,128)} %collective-permute-done.3, pred[]{:T(512)S(6)} %eq.34), kind=kLoop, calls=%fused_computation | loop fusion | flops 25165824 | bytes 67108864 | tf_op jit(solution)/shard_map/jit(_where)/select_n | solution.py:29
  673.7 39.8 %copy.13 = f32[2,16,512,512]{3,1,2,0:T(8,128)} copy(f32[2,16,512,512]{2,3,1,0:T(8,128)} %maximum_select_fusion) | data formatting | bytes 67108864 | tf_op jit(solution)/shard_map/jit(_where)/select_n | solution.py:29
  713.5 20.1 %fusion.54 = f32[2,4,512,512]{3,1,2,0:T(4,128)S(1)} fusion(f32[2,16,512,512]{3,1,2,0:T(8,128)} %copy.13, f32[2,16,16]{1,2,0:T(8,128)S(1)} %bitcast.95, s32[]{:T(128)S(6)} %select_n.129, f32[16,4]{0,1:T(4,128)S(1)} %constant_dynamic-slice_fusion.1), kind=kOutput, calls=%fused_computation.67 | convolution fusion | flops 402653312 | bytes 41949188 | tf_op jit(solution)/shard_map/xwv,xwij->xvij/dot_general | solution.py:77
  733.7 0.7 slice_bitcast_fusion
  734.4 0.0 copy-start.2
  734.4 4.0 collective-permute-start.4
  738.4 89.3 %collective-permute-done.4 = f32[4,512,512]{2,0,1:T(4,128)S(1)} collective-permute-done((f32[4,512,512]{2,0,1:T(4,128)S(1)}, f32[4,512,512]{2,0,1:T(4,128)S(1)}, u32[]{:S(2)}, u32[]{:S(2)}) %collective-permute-start.4) | collective-permute-done | bytes 4194336 | tf_op jit(solution)/shard_map/ppermute | solution.py:25
  827.7 3.0 fusion
  830.7 0.0 collective-permute-start.5
  830.7 1.6 collective-permute-start.6
  832.3 7.1 collective-permute-done.6
  839.5 3.7 collective-permute-start.7
  843.2 4.5 broadcast_select_fusion
  847.7 7.3 collective-permute-done.7
  855.0 8.4 fusion.13
  863.4 8.6 fusion.11
  872.0 9.2 %fusion.9 = f32[1,512,512]{2,0,1:T(1,128)S(1)} fusion(f32[4,512,512]{2,1,0:T(8,128)S(1)} %fusion.11, f32[1,16]{1,0:T(1,128)S(1)} %copy-done, s32[]{:T(128)S(6)} %select_n.129), kind=kOutput, calls=%fused_computation.14 | convolution fusion | flops 12582912 | bytes 5242948 | tf_op jit(solution)/shard_map/w,wik->ik/dot_general | solution.py:86
  881.2 0.1 copy.45
  881.3 0.1 slice_select_fusion
  881.4 3.3 collective-permute-start.8
  884.7 11.0 %collective-permute-done.8 = f32[256,512]{1,0:T(8,128)S(1)} collective-permute-done((f32[256,512]{1,0:T(8,128)S(1)}, f32[256,512]{1,0:T(8,128)S(1)}, u32[]{:S(2)}, u32[]{:S(2)}) %collective-permute-start.8) | collective-permute-done | bytes 524320 | tf_op jit(solution)/shard_map/ppermute | solution.py:19
  895.6 0.1 select_add_fusion
  895.8 1.7 collective-permute-start.9
  897.5 5.5 copy.14
  903.0 0.8 add_bitcast_fusion
  (13 shorter events, 0.1 us)
Async XLA Ops:
  0.6 871.4 %copy-start = (f32[1,16]{1,0:T(1,128)S(1)}, f32[1,16]{1,0:T(1,128)}, u32[]{:S(2)}) copy-start(f32[1,16]{1,0:T(1,128)} %param.13) | copy-start | bytes 196
  0.6 14.0 %collective-permute-start = (f32[128,2,512]{2,1,0:T(2,128)}, f32[128,2,512]{2,1,0:T(2,128)S(1)}, u32[]{:S(2)}, u32[]{:S(2)}) collective-permute-start(f32[128,2,512]{2,1,0:T(2,128)} %bitcast.91), channel_id=1, source_target_pairs={{0,1},{1,0},{2,3},{3,2},{4,5},{5,4},{6,7},{7,6},{8,9},{9,8},{10,11... | collective-permute-start | bytes 1572872 | tf_op jit(solution)/shard_map/ppermute | solution.py:19
  16.9 25.6 %collective-permute-start.1 = (f32[256,2,512]{2,1,0:T(2,128)S(1)}, f32[256,2,512]{2,1,0:T(2,128)S(1)}, u32[]{:S(2)}, u32[]{:S(2)}) collective-permute-start(f32[256,2,512]{2,1,0:T(2,128)S(1)} %maximum_select_fusion.3), channel_id=1, source_target_pairs={{0,2},{2,0},{1,3},{3,1},{4,6},{6,4},{5,7},{7,5},{8,10},{10,8},{9,1... | collective-permute-start | bytes 3145736 | tf_op jit(solution)/shard_map/ppermute | solution.py:19
  22.8 23.2 %copy-start.1 = (f32[1,4,512,512]{3,2,1,0:T(8,128)S(1)}, f32[1,4,512,512]{3,2,1,0:T(8,128)}, u32[]{:S(2)}) copy-start(f32[1,4,512,512]{3,2,1,0:T(8,128)} %param.7) | copy-start | bytes 12582916
  91.8 191.5 %copy-start.4 = (s32[1,16,16]{2,1,0:T(8,128)S(1)}, s32[1,16,16]{2,1,0:T(8,128)}, u32[]{:S(2)}) copy-start(s32[1,16,16]{2,1,0:T(8,128)} %param.10) | copy-start | bytes 3076
  91.8 191.6 %copy-start.3 = (f32[1,2,16,16]{3,2,1,0:T(8,128)S(1)}, f32[1,2,16,16]{3,2,1,0:T(8,128)}, u32[]{:S(2)}) copy-start(f32[1,2,16,16]{3,2,1,0:T(8,128)} %param.11) | copy-start | bytes 6148
  91.8 180.6 %collective-permute-start.2 = (f32[2,4,512,512]{2,3,1,0:T(8,128)}, f32[2,4,512,512]{2,3,1,0:T(8,128)S(1)}, u32[]{:S(2)}, u32[]{:S(2)}) collective-permute-start(f32[2,4,512,512]{2,3,1,0:T(8,128)} %pad_maximum_fusion), channel_id=1, source_target_pairs={{0,1},{1,0},{2,3},{3,2},{4,5},{5,4},{6,7},{7,6},{8,9},{9,8},{10,11... | collective-permute-start | bytes 25165832 | tf_op jit(solution)/shard_map/ppermute | solution.py:19
  280.1 361.1 %collective-permute-start.3 = (f32[2,8,512,512]{2,3,1,0:T(8,128)}, f32[2,8,512,512]{2,3,1,0:T(8,128)}, u32[]{:S(2)}, u32[]{:S(2)}) collective-permute-start(f32[2,8,512,512]{2,3,1,0:T(8,128)} %maximum_select_fusion.1), channel_id=1, source_target_pairs={{0,2},{2,0},{1,3},{3,1},{4,6},{6,4},{5,7},{7,5},{8,10},{10,8},{9,1... | collective-permute-start | bytes 50331656 | tf_op jit(solution)/shard_map/ppermute | solution.py:19
  734.4 96.3 %copy-start.2 = (f32[1,128,512]{2,1,0:T(8,128)S(1)}, f32[1,128,512]{2,1,0:T(8,128)}, u32[]{:S(2)}) copy-start(f32[1,128,512]{2,1,0:T(8,128)} %param.12) | copy-start | bytes 786436
  734.4 93.3 %collective-permute-start.4 = (f32[4,512,512]{2,0,1:T(4,128)S(1)}, f32[4,512,512]{2,0,1:T(4,128)S(1)}, u32[]{:S(2)}, u32[]{:S(2)}) collective-permute-start(f32[4,512,512]{2,0,1:T(4,128)S(1)} %slice_bitcast_fusion), channel_id=1, source_target_pairs={{0,4},{1,5},{2,6},{3,7},{4,8},{5,9},{6,10},{7,11},{8,12},{9,13},{1... | collective-permute-start | bytes 12582920 | tf_op jit(solution)/shard_map/ppermute | solution.py:25
  830.7 12.5 %collective-permute-start.5 = (f32[4,512,512]{2,0,1:T(4,128)}, f32[4,512,512]{2,0,1:T(4,128)}, u32[]{:S(2)}, u32[]{:S(2)}) collective-permute-start(f32[4,512,512]{2,0,1:T(4,128)} %fusion), channel_id=1, source_target_pairs={{0,64},{64,0},{1,65},{65,1},{2,66},{66,2},{3,67},{67,3},{4,68},{68... | collective-permute-start | bytes 12582920 | tf_op jit(solution)/shard_map/ppermute | solution.py:19
  830.7 8.7 collective-permute-start.6
  839.5 15.5 %collective-permute-start.7 = (f32[256,512]{1,0:T(8,128)S(1)}, f32[256,512]{1,0:T(8,128)S(1)}, u32[]{:S(2)}, u32[]{:S(2)}) collective-permute-start(f32[256,512]{1,0:T(8,128)S(1)} %maximum_select_fusion.5), channel_id=1, source_target_pairs={{0,2},{2,0},{1,3},{3,1},{4,6},{6,4},{5,7},{7,5},{8,10},{10,8},{9,1... | collective-permute-start | bytes 1572872 | tf_op jit(solution)/shard_map/ppermute | solution.py:19
  881.4 14.2 %collective-permute-start.8 = (f32[256,512]{1,0:T(8,128)S(1)}, f32[256,512]{1,0:T(8,128)S(1)}, u32[]{:S(2)}, u32[]{:S(2)}) collective-permute-start(f32[256,512]{1,0:T(8,128)S(1)} %slice_select_fusion), channel_id=1, source_target_pairs={{0,2},{2,0},{1,3},{3,1},{4,6},{6,4},{5,7},{7,5},{8,10},{10,8},{9,1... | collective-permute-start | bytes 1572872 | tf_op jit(solution)/shard_map/ppermute | solution.py:19
  895.8 7.2 collective-permute-start.9
where the time goes:
time: 907 us; the launch traced here: 904 us
  waiting for transfers between devices  683 us (75%)
  matrix products  87.8 us (10%)
  other arithmetic  59.8 us (7%)
  local copies, waits for them, and re-layouts  47.9 us (5%)
  starting transfers between devices  23.9 us (3%)
    ppermute x9, waiting for transfers between devices, swapped(): return lax.ppermute(block, axis, route)  594 us
    ppermute x1, waiting for transfers between devices, from_behind(): lax.ppermute(value, axis, [(source, source + steps) for source in range(f...  89.3 us
    select_n x5, other arithmetic, ordered(): jnp.where(is_upper, jnp.concatenate([theirs, mine], axis=axis_dim), jnp.c...  44.4 us
    select_n x1, local copies, waits for them, and re-layouts, ordered(): jnp.where(is_upper, jnp.concatenate([theirs, mine], axis=axis_dim), jnp.c...  39.8 us
    dot_general x2, matrix products, sandwich(): inner = jnp.einsum('wij,jk->wik', blocks, masked, precision=HIGH)  27.3 us
    dot_general x1, matrix products, local(): reduced = jnp.einsum('xwv,xwij->xvij', own_cols, collected, precision=HIGH)  20.1 us
    ppermute x9, starting transfers between devices, swapped(): return lax.ppermute(block, axis, route)  19.9 us
  transfers between devices with their start and end apart: 10, of which 8 were waited for; matrix products, arithmetic and copies ran while one was open for 1% of the time, Pallas kernels for 0%

commit v1 on v0

v1 whole, which is shorter than its diff:
```python
import functools

import jax
import jax.numpy as jnp
from jax import lax
from jax.experimental import pallas as pl
from jax.experimental.pallas import tpu as pltpu
from jax.sharding import PartitionSpec as P

TROW = 32
CH = 32
NE = 16
NK = NE + 3
PSI = NK - 1
AHEAD = 3
MESH = pl.DeviceIdType.MESH
F32, BF16 = jnp.float32, jnp.bfloat16


def halves(value):
    high = value.astype(BF16)
    low = (value - high.astype(F32)).astype(BF16)
    return high, low


def dot3(ah, al, bh, bl):
    dot = functools.partial(jnp.dot, preferred_element_type=F32)
    return dot(ah, bh) + (dot(ah, bl) + dot(al, bh))


def kernel(nsector, env, site, psi, tiles, mask, coef, center, fresh, hpsi,
           own, rcv, f0, f1s, f1r, hbuf, z, zp, abuf, pbuf, q, s1, s2, table,
           load_sem, shift_sem, own_send, own_recv, fwd_send, fwd_recv,
           f1_send, f1_recv, zp_send, zp_recv, out_sem, rs_send, rs_recv):
    section = lax.axis_index("section")
    block = lax.axis_index("block")
    nblock = nsector * 4
    sector = block // 4
    y = block % 4
    base = block - y
    right = (section, base + (y + 1) % 4)
    left = (section, base + (y + 3) % 4)
    above = (section, (block + 4) % nblock)
    below = (section, (block + nblock - 4) % nblock)
    other = (1 - section, block)

    def remote(src, dst, send, recv, to):
        return pltpu.make_async_remote_copy(
            src_ref=src, dst_ref=dst, send_sem=send, recv_sem=recv, device_id=to, device_id_type=MESH)

    def load(k):
        if isinstance(k, int) and k == 0:
            src = site.at[0]
        elif isinstance(k, int) and k == PSI:
            src = psi
        else:
            src = env.at[:, pl.ds(pl.multiple_of((k - 2) * CH, CH), CH), :]
        return pltpu.make_async_copy(src, own.at[k], load_sem.at[k])

    load(0).start()
    lax.fori_loop(2, 2 + NE, lambda k, c: (load(k).start(), c)[1], 0)
    load(PSI).start()

    barrier = pltpu.get_barrier_semaphore()
    for peer in (right, left, above, below, other):
        pl.semaphore_signal(barrier, inc=1, device_id=peer, device_id_type=MESH)
    pl.semaphore_wait(barrier, 5)

    def shift():
        return remote(site.at[1], own.at[1], shift_sem.at[0], shift_sem.at[1], above)

    def to_right(k):
        return remote(own.at[k], rcv.at[2, k], own_send.at[0, k], own_recv.at[0, k], right)

    def to_left(k):
        return remote(own.at[k], rcv.at[0, k], own_send.at[1, k], own_recv.at[1, k], left)

    def on_right(k):
        return remote(rcv.at[2, k, pl.ds(0, 2)], rcv.at[1, k, pl.ds(0, 2)],
                      fwd_send.at[0, k], fwd_recv.at[0, k], right)

    def on_left(k):
        return remote(rcv.at[0, k, pl.ds(2, 2)], rcv.at[1, k, pl.ds(2, 2)],
                      fwd_send.at[1, k], fwd_recv.at[1, k], left)

    def issue(k):
        to_right(k).start()
        to_left(k).start()

    def relay(k):
        to_right(k).wait_recv()
        on_right(k).start()
        to_left(k).wait_recv()
        on_left(k).start()

    def arrived(k):
        on_right(k).wait_recv()
        on_left(k).wait_recv()

    shift().start()
    load(0).wait()
    issue(0)
    load(2).wait()
    issue(2)
    shift().wait_recv()
    issue(1)

    for s in range(2):
        for d in range(4):
            for j in range(4):
                w = ((y + d) % 4) * 4 + j
                for v in range(4):
                    c = coef[0, s, w, y * 4 + v] * mask[0, w, y * 4 + v].astype(F32)
                    table[(s * 4 + v) * 16 + d * 4 + j] = c

    size_here = tiles[sector] * TROW
    size_prev = jnp.where(sector > 0, tiles[jnp.maximum(sector - 1, 0)] * TROW, 0)

    def piece(d, k):
        return own[k] if d == 0 else rcv[d - 1, k]

    def assemble(s, k, rows_kept):
        for d in range(4):
            row0 = pl.multiple_of(((y + d) % 4) * 128, 128)
            v = piece(d, k).reshape(128, 512)
            i = lax.broadcasted_iota(jnp.int32, (128, 512), 0) + row0
            j = lax.broadcasted_iota(jnp.int32, (128, 512), 1)
            v = jnp.where((i < rows_kept) & (j < size_here), v, 0.0)
            t = v.T
            for h, (a, b) in enumerate(zip(halves(v), halves(t))):
                abuf[s * 2 + h, pl.ds(row0, 128), :] = a
                abuf[4 + s * 2 + h, :, pl.ds(row0, 128)] = b

    def f1(e):
        return remote(f1s.at[e], f1r.at[e], f1_send.at[e], f1_recv.at[e], above)

    def mix(e, i):
        k = e + 2

        def rows(r, c):
            span = pl.ds(pl.multiple_of(r * 8, 8), 8)
            acc = [None] * 8
            for d in range(4):
                for j in range(4):
                    x = own[k, j, span, :] if d == 0 else rcv[d - 1, k, j, span, :]
                    for o in range(8):
                        term = table[o * 16 + d * 4 + j] * x
                        acc[o] = term if acc[o] is None else acc[o] + term
            for v in range(4):
                f0[i, v, span, :] = acc[v]
                f1s[e, v, span, :] = acc[4 + v]
            return c

        lax.fori_loop(0, CH // 8, rows, 0)
        f1(e).start()

    def first(s, g):
        def half(t, c):
            lhs = f0[pl.ds(2 * t, 2)] if s == 0 else f1r[pl.ds(4 * g + 2 * t, 2)]
            ah, al = halves(lhs.reshape(256, 512))
            r = dot3(ah, al, abuf[s * 2], abuf[s * 2 + 1])
            for h, part in enumerate(halves(r)):
                part = part.reshape(2, 4, CH, 512)
                for u in range(2):
                    at = pl.multiple_of((g % 2) * 128 + (2 * t + u) * CH, CH)
                    for v in range(4):
                        hbuf[s, h, v, pl.ds(at, CH), :] = part[u, v]
            return c

        lax.fori_loop(0, 2, half, 0)

    def second(half, v):
        cols = pl.ds(half * 256, 256)
        r = None
        for s in range(2):
            t = dot3(abuf[4 + s * 2, :, cols], abuf[5 + s * 2, :, cols], hbuf[s, 0, v], hbuf[s, 1, v])
            r = t if r is None else r + t
        if half == 0:
            z[v] = r
        else:
            z[v] += r

    load(3).wait()
    issue(3)
    relay(0)
    load(4).wait()
    issue(4)
    relay(1)
    arrived(0)
    assemble(0, 0, size_here)
    load(5).wait()
    issue(5)
    relay(2)
    arrived(1)
    assemble(1, 1, size_prev)

    for g in range(4):
        def step(i, c, g=g):
            e = g * 4 + i
            k = e + 3

            @pl.when(e <= NE - 5)
            def _():
                load(k + AHEAD).wait()
                issue(k + AHEAD)

            if g == 3:
                @pl.when(e == NE - 4)
                def _():
                    load(PSI).wait()
                    issue(PSI)

            relay(k)
            arrived(k - 1)
            mix(e, i)
            return c

        lax.fori_loop(0, 4, step, 0)
        if g > 0:
            lax.fori_loop(4 * g - 4, 4 * g, lambda e, c: (f1(e).wait_recv(), c)[1], 0)
            first(1, g - 1)
        if g == 2:
            lax.fori_loop(0, 4, lambda v, c: (second(0, v), c)[1], 0)
        first(0, g)

    arrived(PSI)
    for d in range(4):
        row0 = pl.multiple_of(((y + d) % 4) * 128, 128)
        for h, part in enumerate(halves(piece(d, PSI).reshape(128, 512))):
            pbuf[h, pl.ds(row0, 128), :] = part

    lax.fori_loop(12, 16, lambda e, c: (f1(e).wait_recv(), c)[1], 0)
    first(1, 3)

    def exchange(v):
        return remote(z.at[v], zp.at[v], zp_send.at[v], zp_recv.at[v], other)

    def out(v):
        return pltpu.make_async_copy(z.at[v], fresh.at[v], out_sem.at[v])

    def finish(v, c):
        second(1, v)
        exchange(v).start()
        out(v).start()
        return c

    lax.fori_loop(0, 4, finish, 0)

    def apply_left(v, c):
        exchange(v).wait_recv()
        lh, ll = halves(jnp.where(section == 0, z[v], zp[v]))
        x = dot3(lh, ll, pbuf[0], pbuf[1]) * center[0, y * 4 + v]
        for h, part in enumerate(halves(x)):
            hbuf[0, h, v] = part[:256]
            hbuf[1, h, v] = part[256:]
        rh, rl = halves(jnp.where(section == 0, zp[v], z[v]))
        abuf[2 * v] = rh
        abuf[2 * v + 1] = rl
        return c

    lax.fori_loop(0, 4, apply_left, 0)

    def partial(b):
        rows = pl.ds(pl.multiple_of((b % 2) * 128, 128), 128)
        r = None
        for v in range(4):
            t = dot3(hbuf[b // 2, 0, v, rows, :], hbuf[b // 2, 1, v, rows, :], abuf[2 * v], abuf[2 * v + 1])
            r = t if r is None else r + t
        return r

    hops = [
        remote(q.at[0, 0], s1.at[0], rs_send.at[0], rs_recv.at[0], right),
        remote(q.at[0, 1], s1.at[1], rs_send.at[1], rs_recv.at[1], left),
        remote(q.at[1], s2.at[0], rs_send.at[2], rs_recv.at[2], right),
        remote(q.at[2], s2.at[1], rs_send.at[3], rs_recv.at[3], left),
    ]

    def keep(slot, r):
        q[slot, 0] = r[:, :256]
        q[slot, 1] = r[:, 256:]

    keep(0, partial((y + 2) % 4))
    hops[0].start()
    hops[1].start()
    keep(1, partial((y + 1) % 4))
    hops[0].wait_recv()
    q[1, 0] += s1[0]
    hops[2].start()
    keep(2, partial((y + 3) % 4))
    hops[1].wait_recv()
    q[2, 1] += s1[1]
    hops[3].start()
    keep(3, partial(y))
    hops[2].wait_recv()
    hops[3].wait_recv()
    for t in range(2):
        hpsi[:, pl.ds(t * 256, 256)] = q[3, t] + (s2[0, t] + s2[1, t])

    for hop in hops:
        hop.wait_send()
    shift().wait_send()

    def drain(k, c):
        to_right(k).wait_send()
        to_left(k).wait_send()
        on_right(k).wait_send()
        on_left(k).wait_send()
        return c

    lax.fori_loop(0, NK, drain, 0)
    lax.fori_loop(0, NE, lambda e, c: (f1(e).wait_send(), c)[1], 0)

    def last(v, c):
        exchange(v).wait_send()
        out(v).wait()
        return c

    lax.fori_loop(0, 4, last, 0)


def local(env, site, sector_tiles, mpo_mask, mpo_coef, psi, center_coef):
    spins = site[0].transpose(1, 0, 2).reshape(2, 4, CH, 512)
    anywhere = pl.BlockSpec(memory_space=pl.ANY)
    scalars = pl.BlockSpec(memory_space=pltpu.SMEM)
    dma = pltpu.SemaphoreType.DMA
    fresh, hpsi = pl.pallas_call(
        functools.partial(kernel, sector_tiles.shape[0]),
        out_shape=(
            jax.ShapeDtypeStruct((4, 512, 512), F32),
            jax.ShapeDtypeStruct((128, 512), F32),
        ),
        in_specs=[anywhere, anywhere, anywhere, scalars, scalars, scalars, scalars],
        out_specs=(anywhere, pl.BlockSpec(memory_space=pltpu.VMEM)),
        scratch_shapes=[
            pltpu.VMEM((NK, 4, CH, 512), F32),
            pltpu.VMEM((3, NK, 4, CH, 512), F32),
            pltpu.VMEM((4, 4, CH, 512), F32),
            pltpu.VMEM((NE, 4, CH, 512), F32),
            pltpu.VMEM((NE, 4, CH, 512), F32),
            pltpu.VMEM((2, 2, 4, 256, 512), BF16),
            pltpu.VMEM((4, 512, 512), F32),
            pltpu.VMEM((4, 512, 512), F32),
            pltpu.VMEM((8, 512, 512), BF16),
            pltpu.VMEM((2, 512, 512), BF16),
            pltpu.VMEM((4, 2, 128, 256), F32),
            pltpu.VMEM((2, 128, 256), F32),
            pltpu.VMEM((2, 2, 128, 256), F32),
            pltpu.SMEM((128,), F32),
            dma((NK,)), dma((2,)), dma((2, NK)), dma((2, NK)), dma((2, NK)), dma((2, NK)),
            dma((NE,)), dma((NE,)), dma((4,)), dma((4,)), dma((4,)), dma((4,)), dma((4,)),
        ],
        compiler_params=pltpu.CompilerParams(
            collective_id=0, has_side_effects=True, vmem_limit_bytes=60 << 20
        ),
        name="window",
    )(env[0], spins, psi[0].reshape(4, CH, 512), sector_tiles, mpo_mask, mpo_coef, center_coef)
    return fresh[None], hpsi[None]


def solution(mesh):
    placed = (
        P("section", "block", None, None),
        P("section", "block", None, None),
        P(),
        P("section", None, None),
        P("section", None, None, None),
        P("section", "block", None),
        P("section", None),
    )
    return jax.shard_map(
        local,
        mesh=mesh,
        in_specs=placed,
        out_specs=(P("section", "block", None, None), P("section", "block", None)),
        check_vma=False,
    )
```

time: 907 us -> 216 us (0.24)
  waiting for transfers between devices: 683 us -> 0 us
  Pallas kernels: 0 us -> 205 us
  matrix products: 87.8 us -> 0 us
  other arithmetic: 59.8 us -> 0 us
  local copies, waits for them, and re-layouts: 47.9 us -> 7.33 us
  starting transfers between devices: 23.9 us -> 0 us
    ppermute x10 -> x0, waiting for transfers between devices: 683 us -> none  [the longest x9 594 us: swapped(): return lax.ppermute(block, axis, route)]
    pallas_call x0 -> x1, Pallas kernels: none -> 205 us  [local(): pl.pallas_call(functools.partial(kernel, sector_tiles.shape[0]), out_shap...]
    dot_general x8 -> x0, matrix products: 87.8 us -> none  [the longest x2 27.3 us: sandwich(): inner = jnp.einsum('wij,jk->wik', blocks, masked, precision=HIGH)]
    select_n x8 -> x0, other arithmetic: 49 us -> none  [the longest x5 44.4 us: ordered(): jnp.where(is_upper, jnp.concatenate([theirs, mine], axis=axis_dim), jnp.c...]
    select_n x1 -> x0, local copies, waits for them, and re-layouts: 39.8 us -> none  [ordered(): jnp.where(is_upper, jnp.concatenate([theirs, mine], axis=axis_dim), jnp.c...]
    ppermute x10 -> x0, starting transfers between devices: 23.9 us -> none  [the longest x9 19.9 us: swapped(): return lax.ppermute(block, axis, route)]
  transfers between devices with their start and end apart: 10 -> 0, of which waited for: 8 -> 0; matrix products, arithmetic and copies ran while one was open for 1% -> 0% of each run, Pallas kernels for 0% -> 0%
where the time goes in v1:
time: 216 us; the launch traced here: 213 us
  Pallas kernels  205 us (95%)
  local copies, waits for them, and re-layouts  7.33 us (3%)
    pallas_call x1, Pallas kernels, local(): pl.pallas_call(functools.partial(kernel, sector_tiles.shape[0]), out_shap...  205 us
    unnamed x4, local copies, waits for them, and re-layouts  5.39 us

profile of v1, /device:TPU:6, one launch (start us, length us, event | category | flops | bytes accessed | tf_op | source)
XLA Modules:
  0.0 213.3 jit_solution(15885403734773098539)
XLA Ops:
  0.6 1.9 copy.9
  2.6 205.4 %window.1 = (f32[4,512,512]{2,1,0:T(8,128)}, f32[128,512]{1,0:T(8,128)}) custom-call(f32[4,512,512]{2,1,0:T(8,128)} %bitcast.8, f32[2,4,32,512]{3,2,1,0:T(8,128)} %bitcast.10, f32[4,32,512]{2,1,0:T(8,128)} %bitcast.12, s32[16]{0:T(128)} %tiles.1, s32[1,16,16]{2,1,0:T(8,128)} %mask.1, f32[1,2,16,16]{3,2,1,0:T(8,128)} %coef.1, f32[1,16]{1,0:T(1,128)} %center.1), custom_call_target="tpu_custom_call" | custom-call | tf_op jit(solution)/shard_map/window/pallas_call | solution.py:326
  207.9 0.0 copy-start
  208.0 4.7 %copy.12 = f32[1,4,512,512]{3,2,1,0:T(8,128)} copy(f32[1,4,512,512]{3,2,1,0:T(8,128)} %bitcast.9) | data formatting | bytes 8388608
  212.6 0.0 copy-done
  212.6 0.7 copy.13
Async XLA Ops:
  207.9 4.7 %copy-start = (f32[128,512]{1,0:T(8,128)S(1)}, f32[128,512]{1,0:T(8,128)}, u32[]{:S(2)}) copy-start(f32[128,512]{1,0:T(8,128)} %get-tuple-element.5) | copy-start | bytes 786436

commit v2 on v1

v2 whole, which is shorter than its diff:
```python
import functools

import jax
import jax.numpy as jnp
from jax import lax
from jax.experimental import pallas as pl
from jax.experimental.pallas import tpu as pltpu
from jax.sharding import PartitionSpec as P

TROW = 32
CH = 32
UR = 16
NL = 8
LOW = (0, 1, 2, 9, 10, 11, 12, 13)
A0, A1, PSI = 3, 8, 14
SHARED = (4, 5, 6, 7)
NK = 15
MESH = pl.DeviceIdType.MESH
F32, BF16 = jnp.float32, jnp.bfloat16


def halves(value):
    high = value.astype(BF16)
    low = (value - high.astype(F32)).astype(BF16)
    return high, low


def dot3(ah, al, bh, bl):
    dot = functools.partial(jnp.dot, preferred_element_type=F32)
    return dot(ah, bh) + (dot(ah, bl) + dot(al, bh))


def kernel(nsector, env, site, psi, tiles, mask, coef, center, fresh, hpsi,
           own, rcv, f0, f1s, f1r, up, pack, got, fu, back0, back1, hbuf, z, zp, abuf, pbuf, q, s1, s2, table, place,
           load_sem, up_sem, shift_sem, own_send, own_recv, fwd_send, fwd_recv, f1_send, f1_recv,
           sh_send, sh_recv, bk_send, bk_recv, zp_send, zp_recv, out_sem, rs_send, rs_recv):
    section = lax.axis_index("section")
    block = lax.axis_index("block")
    sector = block // 4
    y = block % 4
    base = block - y
    right = (section, base + (y + 1) % 4)
    left = (section, base + (y + 3) % 4)
    other = (1 - section, block)

    def ring(distance):
        return (section, ((sector + distance + nsector) % nsector) * 4 + y)

    above = ring(1)

    def remote(src, dst, send, recv, to):
        return pltpu.make_async_remote_copy(
            src_ref=src, dst_ref=dst, send_sem=send, recv_sem=recv, device_id=to, device_id_type=MESH)

    def loop(lo, hi, body):
        lax.fori_loop(lo, hi, lambda i, c: (body(i), c)[1], 0)

    def load(k):
        if k == A0:
            src = site.at[0]
        elif k == PSI:
            src = psi
        else:
            src = env.at[:, pl.ds(LOW.index(k) * CH, CH), :]
        return pltpu.make_async_copy(src, own.at[k], load_sem.at[k])

    def load_up(u):
        rows = pl.ds(pl.multiple_of(256 + u * UR, UR), UR)
        return pltpu.make_async_copy(env.at[:, rows, :], up.at[u], up_sem.at[u])

    load(0).start()
    loop(0, nsector, lambda u: load_up(u).start())
    for k in LOW[1:] + (A0, PSI):
        load(k).start()

    barrier = pltpu.get_barrier_semaphore()
    for peer in (right, left, other):
        pl.semaphore_signal(barrier, inc=1, device_id=peer, device_id_type=MESH)
    loop(1, nsector, lambda d: pl.semaphore_signal(barrier, inc=1, device_id=ring(d), device_id_type=MESH))
    pl.semaphore_wait(barrier, nsector + 2)

    def shift():
        return remote(site.at[1], own.at[A1], shift_sem.at[0], shift_sem.at[1], above)

    def rows_of(k):
        return pl.ds(0, UR if k == SHARED[3] else CH)

    def to_right(k):
        r = rows_of(k)
        return remote(own.at[k, :, r], rcv.at[2, k, :, r], own_send.at[0, k], own_recv.at[0, k], right)

    def to_left(k):
        r = rows_of(k)
        return remote(own.at[k, :, r], rcv.at[0, k, :, r], own_send.at[1, k], own_recv.at[1, k], left)

    def on_right(k):
        r = rows_of(k)
        return remote(rcv.at[2, k, pl.ds(0, 2), r], rcv.at[1, k, pl.ds(0, 2), r],
                      fwd_send.at[0, k], fwd_recv.at[0, k], right)

    def on_left(k):
        r = rows_of(k)
        return remote(rcv.at[0, k, pl.ds(2, 2), r], rcv.at[1, k, pl.ds(2, 2), r],
                      fwd_send.at[1, k], fwd_recv.at[1, k], left)

    def issue(k):
        if k in LOW + (A0, PSI):
            load(k).wait()
        to_right(k).start()
        to_left(k).start()

    def relay(k):
        to_right(k).wait_recv()
        on_right(k).start()
        to_left(k).wait_recv()
        on_left(k).start()

    def arrived(k):
        on_right(k).wait_recv()
        on_left(k).wait_recv()

    issue(0)

    start = 0
    for i in range(nsector):
        count = jnp.maximum(2 * (tiles[i] - 8), 0)
        place[i] = start % 16
        place[16 + i] = count
        start = start + count

    def share(d):
        return remote(pack.at[d], got.at[d], sh_send.at[d], sh_recv.at[d], ring(d))

    loop(0, nsector, lambda u: load_up(u).wait())

    def unit_for(d):
        return (sector + d + 16 - place[sector]) % 16

    got[0] = up[unit_for(0)]

    def send_share(d):
        pack[d] = up[unit_for(d)]
        share(d).start()

    loop(1, nsector, send_share)
    shift().start()
    issue(1)
    issue(2)

    for s in range(2):
        for d in range(4):
            for j in range(4):
                w = ((y + d) % 4) * 4 + j
                for v in range(4):
                    c = coef[0, s, w, y * 4 + v] * mask[0, w, y * 4 + v].astype(F32)
                    table[(s * 4 + v) * 16 + d * 4 + j] = c

    rank = 0
    chosen = [0] * 8
    for d in range(nsector):
        home = (sector - d + 16) % 16
        valid = (sector + 16 - place[home]) % 16 < place[16 + home]
        place[32 + d] = jnp.where(valid, rank, 0)
        for j in range(7):
            chosen[j] = jnp.where(valid & (rank == j), d, chosen[j])
        rank = rank + valid.astype(jnp.int32)

    size_here = tiles[sector] * TROW
    before = (sector + nsector - 1) % nsector
    size_prev = jnp.where(sector > 0, tiles[before] * TROW, 0)

    def piece(d, k):
        return own[k] if d == 0 else rcv[d - 1, k]

    def assemble(s, k, rows_kept):
        arrived(k)
        for d in range(4):
            row0 = pl.multiple_of(((y + d) % 4) * 128, 128)
            v = piece(d, k).reshape(128, 512)
            i = lax.broadcasted_iota(jnp.int32, (128, 512), 0) + row0
            j = lax.broadcasted_iota(jnp.int32, (128, 512), 1)
            v = jnp.where((i < rows_kept) & (j < size_here), v, 0.0)
            t = v.T
            for h, (a, b) in enumerate(zip(halves(v), halves(t))):
                abuf[s * 2 + h, pl.ds(row0, 128), :] = a
                abuf[4 + s * 2 + h, :, pl.ds(row0, 128)] = b

    def f1(e):
        return remote(f1s.at[e], f1r.at[e], f1_send.at[e], f1_recv.at[e], above)

    def mix(k, nrows, put):
        arrived(k)

        def rows(r):
            span = pl.ds(pl.multiple_of(r * 8, 8), 8)
            acc = [None] * 8
            for d in range(4):
                for j in range(4):
                    x = own[k, j, span, :] if d == 0 else rcv[d - 1, k, j, span, :]
                    for o in range(8):
                        term = table[o * 16 + d * 4 + j] * x
                        acc[o] = term if acc[o] is None else acc[o] + term
            put(r, acc)

        loop(0, nrows // 8, rows)

    def mix_low(e):
        def put(r, acc):
            span = pl.ds(pl.multiple_of(r * 8, 8), 8)
            for v in range(4):
                f0[e, v, span, :] = acc[v]
                f1s[e, v, span, :] = acc[4 + v]

        mix(LOW[e], CH, put)
        f1(e).start()

    def mix_shared(n):
        def put(r, acc):
            span = pl.ds(pl.multiple_of((r % 2) * 8, 8), 8)
            for v in range(4):
                fu[0, 2 * n + r // 2, v, span, :] = acc[v]
                fu[1, 2 * n + r // 2, v, span, :] = acc[4 + v]

        mix(SHARED[n], UR if n == 3 else CH, put)

    back = (back0, back1)

    def give(s, d):
        source = pack if s == 0 else up
        to = ring(nsector - d + s)
        return remote(source.at[d], back[s].at[d], bk_send.at[s, d], bk_recv.at[s, d], to)

    def give_back():
        loop(1, nsector, lambda d: share(d).wait_send())
        back0[0] = fu[0, place[32]]
        back1[1] = fu[1, place[33]]

        def send(s, d):
            (pack if s == 0 else up)[d] = fu[s, place[32 + d]]
            give(s, d).start()

        send(1, 0)
        send(0, 1)

        def both(d):
            send(0, d)
            send(1, d)

        loop(2, nsector, both)

    def given(s):
        send_range = range(1, 2) if s == 0 else range(0, 1)
        for d in send_range:
            give(s, d).wait_recv()
        loop(2, nsector, lambda d: give(s, d).wait_recv())

    def store_h(group, s, r, count, rows, at):
        for h, part in enumerate(halves(r)):
            part = part.reshape(count, 4, rows, 512)
            for u in range(count):
                for v in range(4):
                    hbuf[group, s, h, v, pl.ds(pl.multiple_of(at + u * rows, 16), rows), :] = part[u, v]

    def first_low(s, g):
        def half(t):
            at = 4 * g + 2 * t
            lhs = (f0 if s == 0 else f1r)[pl.ds(at, 2)]
            ah, al = halves(lhs.reshape(256, 512))
            store_h(0, s, dot3(ah, al, abuf[s * 2], abuf[s * 2 + 1]), 2, CH, at * CH)

        loop(0, 2, half)

    def first_shared(s):
        home = sector if s == 0 else before

        def quarter(t):
            units = [back[s][(4 * t + i + place[home] + 16 - home) % 16] for i in range(4)]
            ah, al = halves(jnp.concatenate([u.reshape(64, 512) for u in units], axis=0))
            store_h(1, s, dot3(ah, al, abuf[s * 2], abuf[s * 2 + 1]), 4, UR, t * 64)

        loop(0, 4, quarter)

    def second(group, v):
        cols = pl.ds(group * 256, 256)
        r = None
        for s in range(2):
            t = dot3(abuf[4 + s * 2, :, cols], abuf[5 + s * 2, :, cols], hbuf[group, s, 0, v], hbuf[group, s, 1, v])
            r = t if r is None else r + t
        if group == 1:
            z[v] = r
        else:
            z[v] += r

    relay(0)
    issue(A0)
    relay(1)
    mix_low(0)
    relay(2)
    mix_low(1)
    loop(1, nsector, lambda d: share(d).wait_recv())
    for n in range(4):
        for t in range(1 if n == 3 else 2):
            own[SHARED[n], :, pl.ds(t * UR, UR), :] = got[chosen[2 * n + t]]
    issue(4)
    issue(5)
    relay(3)
    mix_low(2)
    issue(6)
    relay(4)
    assemble(0, A0, size_here)
    issue(7)
    relay(5)
    mix_shared(0)
    shift().wait_recv()
    issue(A1)
    relay(6)
    mix_shared(1)
    issue(9)
    relay(7)
    mix_shared(2)
    issue(10)
    relay(8)
    mix_shared(3)
    give_back()
    issue(11)
    relay(9)
    assemble(1, A1, size_prev)
    issue(12)
    relay(10)
    mix_low(3)
    issue(13)
    first_low(0, 0)
    relay(11)
    mix_low(4)
    issue(14)
    relay(12)
    mix_low(5)
    relay(13)
    mix_low(6)
    given(0)
    first_shared(0)
    relay(14)
    mix_low(7)
    first_low(0, 1)
    given(1)
    first_shared(1)
    loop(0, 4, lambda v: second(1, v))

    arrived(PSI)
    for d in range(4):
        row0 = pl.multiple_of(((y + d) % 4) * 128, 128)
        for h, part in enumerate(halves(piece(d, PSI).reshape(128, 512))):
            pbuf[h, pl.ds(row0, 128), :] = part

    for g in range(2):
        loop(4 * g, 4 * g + 4, lambda e: f1(e).wait_recv())
        first_low(1, g)

    def exchange(v):
        return remote(z.at[v], zp.at[v], zp_send.at[v], zp_recv.at[v], other)

    def out(v):
        return pltpu.make_async_copy(z.at[v], fresh.at[v], out_sem.at[v])

    def finish(v):
        second(0, v)
        exchange(v).start()
        out(v).start()

    loop(0, 4, finish)

    def apply_left(v):
        exchange(v).wait_recv()
        lh, ll = halves(jnp.where(section == 0, z[v], zp[v]))
        x = dot3(lh, ll, pbuf[0], pbuf[1]) * center[0, y * 4 + v]
        for h, part in enumerate(halves(x)):
            hbuf[0, 0, h, v] = part[:256]
            hbuf[0, 1, h, v] = part[256:]
        rh, rl = halves(jnp.where(section == 0, zp[v], z[v]))
        abuf[2 * v] = rh
        abuf[2 * v + 1] = rl

    loop(0, 4, apply_left)

    def partial(b):
        rows = pl.ds(pl.multiple_of((b % 2) * 128, 128), 128)
        r = None
        for v in range(4):
            t = dot3(hbuf[0, b // 2, 0, v, rows, :], hbuf[0, b // 2, 1, v, rows, :], abuf[2 * v], abuf[2 * v + 1])
            r = t if r is None else r + t
        return r

    hops = [
        remote(q.at[0, 0], s1.at[0], rs_send.at[0], rs_recv.at[0], right),
        remote(q.at[0, 1], s1.at[1], rs_send.at[1], rs_recv.at[1], left),
        remote(q.at[1], s2.at[0], rs_send.at[2], rs_recv.at[2], right),
        remote(q.at[2], s2.at[1], rs_send.at[3], rs_recv.at[3], left),
    ]

    def keep(slot, r):
        q[slot, 0] = r[:, :256]
        q[slot, 1] = r[:, 256:]

    keep(0, partial((y + 2) % 4))
    hops[0].start()
    hops[1].start()
    keep(1, partial((y + 1) % 4))
    hops[0].wait_recv()
    q[1, 0] += s1[0]
    hops[2].start()
    keep(2, partial((y + 3) % 4))
    hops[1].wait_recv()
    q[2, 1] += s1[1]
    hops[3].start()
    keep(3, partial(y))
    hops[2].wait_recv()
    hops[3].wait_recv()
    for t in range(2):
        hpsi[:, pl.ds(t * 256, 256)] = q[3, t] + (s2[0, t] + s2[1, t])

    for hop in hops:
        hop.wait_send()
    shift().wait_send()
    for k in range(NK):
        to_right(k).wait_send()
        to_left(k).wait_send()
        on_right(k).wait_send()
        on_left(k).wait_send()
    loop(0, NL, lambda e: f1(e).wait_send())
    give(1, 0).wait_send()
    give(0, 1).wait_send()

    def gone(d):
        give(0, d).wait_send()
        give(1, d).wait_send()

    loop(2, nsector, gone)

    def last(v):
        exchange(v).wait_send()
        out(v).wait()

    loop(0, 4, last)


def local(env, site, sector_tiles, mpo_mask, mpo_coef, psi, center_coef):
    spins = site[0].transpose(1, 0, 2).reshape(2, 4, CH, 512)
    anywhere = pl.BlockSpec(memory_space=pl.ANY)
    scalars = pl.BlockSpec(memory_space=pltpu.SMEM)
    dma = pltpu.SemaphoreType.DMA
    fresh, hpsi = pl.pallas_call(
        functools.partial(kernel, sector_tiles.shape[0]),
        out_shape=(
            jax.ShapeDtypeStruct((4, 512, 512), F32),
            jax.ShapeDtypeStruct((128, 512), F32),
        ),
        in_specs=[anywhere, anywhere, anywhere, scalars, scalars, scalars, scalars],
        out_specs=(anywhere, pl.BlockSpec(memory_space=pltpu.VMEM)),
        scratch_shapes=[
            pltpu.VMEM((NK, 4, CH, 512), F32),
            pltpu.VMEM((3, NK, 4, CH, 512), F32),
            pltpu.VMEM((NL, 4, CH, 512), F32),
            pltpu.VMEM((NL, 4, CH, 512), F32),
            pltpu.VMEM((NL, 4, CH, 512), F32),
            pltpu.VMEM((16, 4, UR, 512), F32),
            pltpu.VMEM((16, 4, UR, 512), F32),
            pltpu.VMEM((16, 4, UR, 512), F32),
            pltpu.VMEM((2, 7, 4, UR, 512), F32),
            pltpu.VMEM((16, 4, UR, 512), F32),
            pltpu.VMEM((16, 4, UR, 512), F32),
            pltpu.VMEM((2, 2, 2, 4, 256, 512), BF16),
            pltpu.VMEM((4, 512, 512), F32),
            pltpu.VMEM((4, 512, 512), F32),
            pltpu.VMEM((8, 512, 512), BF16),
            pltpu.VMEM((2, 512, 512), BF16),
            pltpu.VMEM((4, 2, 128, 256), F32),
            pltpu.VMEM((2, 128, 256), F32),
            pltpu.VMEM((2, 2, 128, 256), F32),
            pltpu.SMEM((128,), F32),
            pltpu.SMEM((48,), jnp.int32),
            dma((NK,)), dma((16,)), dma((2,)), dma((2, NK)), dma((2, NK)), dma((2, NK)), dma((2, NK)),
            dma((NL,)), dma((NL,)), dma((16,)), dma((16,)), dma((2, 16)), dma((2, 16)),
            dma((4,)), dma((4,)), dma((4,)), dma((4,)), dma((4,)),
        ],
        compiler_params=pltpu.CompilerParams(
            collective_id=0, has_side_effects=True, vmem_limit_bytes=62 << 20
        ),
        name="window",
    )(env[0], spins, psi[0].reshape(4, CH, 512), sector_tiles, mpo_mask, mpo_coef, center_coef)
    return fresh[None], hpsi[None]


def solution(mesh):
    placed = (
        P("section", "block", None, None),
        P("section", "block", None, None),
        P(),
        P("section", None, None),
        P("section", None, None, None),
        P("section", "block", None),
        P("section", None),
    )
    return jax.shard_map(
        local,
        mesh=mesh,
        in_specs=placed,
        out_specs=(P("section", "block", None, None), P("section", "block", None)),
        check_vma=False,
    )
```

time: 216 us -> 213 us (0.986)
  Pallas kernels: 205 us -> 201 us
    pallas_call x1, Pallas kernels: 205 us -> 201 us  [local(): pl.pallas_call(functools.partial(kernel, sector_tiles.shape[0]), out_shap...]
where the time goes in v2:
time: 213 us; the launch traced here: 209 us
  Pallas kernels  201 us (94%)
  local copies, waits for them, and re-layouts  7.33 us (3%)
    pallas_call x1, Pallas kernels, local(): pl.pallas_call(functools.partial(kernel, sector_tiles.shape[0]), out_shap...  201 us
    unnamed x4, local copies, waits for them, and re-layouts  5.39 us

profile of v2, /device:TPU:6, one launch (start us, length us, event | category | flops | bytes accessed | tf_op | source)
XLA Modules:
  0.0 209.1 jit_solution(226388147745382802)
XLA Ops:
  0.6 1.9 copy.9
  2.6 201.1 %window.1 = (f32[4,512,512]{2,1,0:T(8,128)}, f32[128,512]{1,0:T(8,128)}) custom-call(f32[4,512,512]{2,1,0:T(8,128)} %bitcast.8, f32[2,4,32,512]{3,2,1,0:T(8,128)} %bitcast.10, f32[4,32,512]{2,1,0:T(8,128)} %bitcast.12, s32[16]{0:T(128)} %tiles.1, s32[1,16,16]{2,1,0:T(8,128)} %mask.1, f32[1,2,16,16]{3,2,1,0:T(8,128)} %coef.1, f32[1,16]{1,0:T(1,128)} %center.1), custom_call_target="tpu_custom_call" | custom-call | tf_op jit(solution)/shard_map/window/pallas_call | solution.py:451
  203.7 0.0 copy-start
  203.7 4.7 %copy.12 = f32[1,4,512,512]{3,2,1,0:T(8,128)} copy(f32[1,4,512,512]{3,2,1,0:T(8,128)} %bitcast.9) | data formatting | bytes 8388608
  208.4 0.0 copy-done
  208.4 0.7 copy.13
Async XLA Ops:
  203.7 4.7 %copy-start = (f32[128,512]{1,0:T(8,128)S(1)}, f32[128,512]{1,0:T(8,128)}, u32[]{:S(2)}) copy-start(f32[128,512]{1,0:T(8,128)} %get-tuple-element.5) | copy-start | bytes 786436

commit v3 on v2

--- a/solution.py
+++ b/solution.py
@@ -11,10 +11,11 @@
 CH = 32
 UR = 16
 NL = 8
-LOW = (0, 1, 2, 9, 10, 11, 12, 13)
-A0, A1, PSI = 3, 8, 14
-SHARED = (4, 5, 6, 7)
+LOW = (0, 1, 2, 7, 9, 11, 12, 13)
+A0, A1, PSI = 8, 10, 14
+SHARED = (3, 4, 5, 6)
 NK = 15
+ORDER = (1, 4, 15, 12, 5, 11, 3, 13, 2, 8, 6, 9, 14, 7, 10)
 MESH = pl.DeviceIdType.MESH
 F32, BF16 = jnp.float32, jnp.bfloat16
 
@@ -83,7 +84,7 @@
         return remote(site.at[1], own.at[A1], shift_sem.at[0], shift_sem.at[1], above)
 
     def rows_of(k):
-        return pl.ds(0, UR if k == SHARED[3] else CH)
+        return pl.ds(0, CH)
 
     def to_right(k):
         r = rows_of(k)
@@ -142,7 +143,8 @@
         pack[d] = up[unit_for(d)]
         share(d).start()
 
-    loop(1, nsector, send_share)
+    for d in ORDER:
+        send_share(d)
     shift().start()
     issue(1)
     issue(2)
@@ -217,42 +219,41 @@
     def mix_shared(n):
         def put(r, acc):
             span = pl.ds(pl.multiple_of((r % 2) * 8, 8), 8)
-            for v in range(4):
-                fu[0, 2 * n + r // 2, v, span, :] = acc[v]
-                fu[1, 2 * n + r // 2, v, span, :] = acc[4 + v]
-
-        mix(SHARED[n], UR if n == 3 else CH, put)
+            for o in range(8):
+                for c in range(2):
+                    unit = n % 2 * 4 + 2 * c + r // 2
+                    fu[n // 2, o // 4, unit, o % 4, span, :] = acc[o][:, c * 256:c * 256 + 256]
+
+        mix(SHARED[n], CH, put)
 
     back = (back0, back1)
 
-    def give(s, d):
+    def give(h, s, d):
         source = pack if s == 0 else up
         to = ring(nsector - d + s)
-        return remote(source.at[d], back[s].at[d], bk_send.at[s, d], bk_recv.at[s, d], to)
-
-    def give_back():
-        loop(1, nsector, lambda d: share(d).wait_send())
-        back0[0] = fu[0, place[32]]
-        back1[1] = fu[1, place[33]]
+        cols = pl.ds(h * 256, 256)
+        return remote(source.at[d, :, :, cols], back[s].at[d, :, :, cols], bk_send.at[h, s, d], bk_recv.at[h, s, d], to)
+
+    def give_back(h):
+        cols = pl.ds(h * 256, 256)
+        if h == 0:
+            loop(1, nsector, lambda d: share(d).wait_send())
+        back0[0, :, :, cols] = fu[h, 0, place[32]]
+        back1[1, :, :, cols] = fu[h, 1, place[33]]
 
         def send(s, d):
-            (pack if s == 0 else up)[d] = fu[s, place[32 + d]]
-            give(s, d).start()
-
-        send(1, 0)
-        send(0, 1)
-
-        def both(d):
-            send(0, d)
-            send(1, d)
-
-        loop(2, nsector, both)
+            (pack if s == 0 else up)[d, :, :, cols] = fu[h, s, place[32 + d]]
+            give(h, s, d).start()
+
+        for d in ORDER:
+            send(0, 16 - d)
+        for d in ORDER:
+            send(1, (17 - d) % 16)
 
     def given(s):
-        send_range = range(1, 2) if s == 0 else range(0, 1)
-        for d in send_range:
-            give(s, d).wait_recv()
-        loop(2, nsector, lambda d: give(s, d).wait_recv())
+        for h in range(2):
+            give(h, s, 1 - s).wait_recv()
+            loop(2, nsector, lambda d, h=h: give(h, s, d).wait_recv())
 
     def store_h(group, s, r, count, rows, at):
         for h, part in enumerate(halves(r)):
@@ -286,52 +287,54 @@
         for s in range(2):
             t = dot3(abuf[4 + s * 2, :, cols], abuf[5 + s * 2, :, cols], hbuf[group, s, 0, v], hbuf[group, s, 1, v])
             r = t if r is None else r + t
-        if group == 1:
+        if group == 0:
             z[v] = r
         else:
             z[v] += r
 
     relay(0)
-    issue(A0)
     relay(1)
     mix_low(0)
     relay(2)
     mix_low(1)
     loop(1, nsector, lambda d: share(d).wait_recv())
     for n in range(4):
-        for t in range(1 if n == 3 else 2):
-            own[SHARED[n], :, pl.ds(t * UR, UR), :] = got[chosen[2 * n + t]]
+        for i in range(4):
+            own[SHARED[n], :, pl.ds(i % 2 * UR, UR), pl.ds(i // 2 * 256, 256)] = got[
+                chosen[n % 2 * 4 + i], :, :, pl.ds(n // 2 * 256, 256)]
+    issue(3)
     issue(4)
     issue(5)
+    mix_low(2)
     relay(3)
-    mix_low(2)
     issue(6)
     relay(4)
-    assemble(0, A0, size_here)
+    mix_shared(0)
     issue(7)
     relay(5)
-    mix_shared(0)
-    shift().wait_recv()
-    issue(A1)
+    mix_shared(1)
+    issue(8)
+    give_back(0)
     relay(6)
-    mix_shared(1)
+    mix_shared(2)
     issue(9)
     relay(7)
-    mix_shared(2)
+    mix_shared(3)
+    give_back(1)
+    shift().wait_recv()
     issue(10)
     relay(8)
-    mix_shared(3)
-    give_back()
+    mix_low(3)
     issue(11)
     relay(9)
-    assemble(1, A1, size_prev)
+    assemble(0, A0, size_here)
     issue(12)
     relay(10)
-    mix_low(3)
+    mix_low(4)
     issue(13)
     first_low(0, 0)
     relay(11)
-    mix_low(4)
+    assemble(1, A1, size_prev)
     issue(14)
     relay(12)
     mix_low(5)
@@ -342,10 +345,6 @@
     relay(14)
     mix_low(7)
     first_low(0, 1)
-    given(1)
-    first_shared(1)
-    loop(0, 4, lambda v: second(1, v))
-
     arrived(PSI)
     for d in range(4):
         row0 = pl.multiple_of(((y + d) % 4) * 128, 128)
@@ -355,6 +354,9 @@
     for g in range(2):
         loop(4 * g, 4 * g + 4, lambda e: f1(e).wait_recv())
         first_low(1, g)
+    loop(0, 4, lambda v: second(0, v))
+    given(1)
+    first_shared(1)
 
     def exchange(v):
         return remote(z.at[v], zp.at[v], zp_send.at[v], zp_recv.at[v], other)
@@ -363,7 +365,7 @@
         return pltpu.make_async_copy(z.at[v], fresh.at[v], out_sem.at[v])
 
     def finish(v):
-        second(0, v)
+        second(1, v)
         exchange(v).start()
         out(v).start()
 
@@ -427,20 +429,31 @@
         on_right(k).wait_send()
         on_left(k).wait_send()
     loop(0, NL, lambda e: f1(e).wait_send())
-    give(1, 0).wait_send()
-    give(0, 1).wait_send()
-
-    def gone(d):
-        give(0, d).wait_send()
-        give(1, d).wait_send()
-
-    loop(2, nsector, gone)
+    for h in range(2):
+        for s in range(2):
+            give(h, s, 1 - s).wait_send()
+            loop(2, nsector, lambda d, h=h, s=s: give(h, s, d).wait_send())
 
     def last(v):
         exchange(v).wait_send()
         out(v).wait()
 
     loop(0, 4, last)
+
+
+def settle(src, dst, held, came, gone):
+    def part(ref, i):
+        return ref.at[i // 4, pl.ds(i % 4 * 128, 128), :]
+
+    incoming = [pltpu.make_async_copy(part(src, i), held.at[i], came.at[i]) for i in range(16)]
+    outgoing = [pltpu.make_async_copy(held.at[i], part(dst, i), gone.at[i]) for i in range(16)]
+    for copy in incoming:
+        copy.start()
+    for i in range(16):
+        incoming[i].wait()
+        outgoing[i].start()
+    for copy in outgoing:
+        copy.wait()
 
 
 def local(env, site, sector_tiles, mpo_mask, mpo_coef, psi, center_coef):
@@ -465,7 +478,7 @@
             pltpu.VMEM((16, 4, UR, 512), F32),
             pltpu.VMEM((16, 4, UR, 512), F32),
             pltpu.VMEM((16, 4, UR, 512), F32),
-            pltpu.VMEM((2, 7, 4, UR, 512), F32),
+            pltpu.VMEM((2, 2, 8, 4, UR, 256), F32),
             pltpu.VMEM((16, 4, UR, 512), F32),
             pltpu.VMEM((16, 4, UR, 512), F32),
             pltpu.VMEM((2, 2, 2, 4, 256, 512), BF16),
@@ -479,7 +492,7 @@
             pltpu.SMEM((128,), F32),
             pltpu.SMEM((48,), jnp.int32),
             dma((NK,)), dma((16,)), dma((2,)), dma((2, NK)), dma((2, NK)), dma((2, NK)), dma((2, NK)),
-            dma((NL,)), dma((NL,)), dma((16,)), dma((16,)), dma((2, 16)), dma((2, 16)),
+            dma((NL,)), dma((NL,)), dma((16,)), dma((16,)), dma((2, 2, 16)), dma((2, 2, 16)),
             dma((4,)), dma((4,)), dma((4,)), dma((4,)), dma((4,)),
         ],
         compiler_params=pltpu.CompilerParams(
@@ -487,6 +500,14 @@
         ),
         name="window",
     )(env[0], spins, psi[0].reshape(4, CH, 512), sector_tiles, mpo_mask, mpo_coef, center_coef)
+    fresh = pl.pallas_call(
+        settle,
+        out_shape=jax.ShapeDtypeStruct((4, 512, 512), F32),
+        in_specs=[anywhere],
+        out_specs=anywhere,
+        scratch_shapes=[pltpu.VMEM((16, 128, 512), F32), dma((16,)), dma((16,))],
+        name="settle",
+    )(fresh)
     return fresh[None], hpsi[None]
 
 

time: 213 us -> 190 us (0.89)
  Pallas kernels: 201 us -> 184 us
  local copies, waits for them, and re-layouts: 7.33 us -> 2.65 us
    pallas_call x1, Pallas kernels: 201 us -> 180 us  [local(): pl.pallas_call(functools.partial(kernel, sector_tiles.shape[0]), out_shap...]
    unnamed x4 -> x3, local copies, waits for them, and re-layouts: 5.39 us -> 0.71 us
    pallas_call x0 -> x1, Pallas kernels: none -> 3.89 us  [local(): pl.pallas_call(settle, out_shape=jax.ShapeDtypeStruct((4, 512, 512), F32)...]
where the time goes in v3:
time: 190 us; the launch traced here: 187 us
  Pallas kernels  184 us (97%)
  local copies, waits for them, and re-layouts  2.65 us (1%)
    pallas_call x1, Pallas kernels, local(): pl.pallas_call(functools.partial(kernel, sector_tiles.shape[0]), out_shap...  180 us
    pallas_call x1, Pallas kernels, local(): pl.pallas_call(settle, out_shape=jax.ShapeDtypeStruct((4, 512, 512), F32)...  3.89 us

profile of v3, /device:TPU:6, one launch (start us, length us, event | category | flops | bytes accessed | tf_op | source)
XLA Modules:
  0.0 187.2 jit_solution(11584630640011923489)
XLA Ops:
  0.6 1.9 %copy.9 = f32[2,128,512]{2,1,0:T(8,128)} copy(f32[2,128,512]{2,0,1:T(2,128)} %bitcast.11) | data formatting | bytes 1048576 | tf_op jit(solution)/shard_map/transpose | solution.py:460
  2.6 180.0 %window.1 = (f32[4,512,512]{2,1,0:T(8,128)}, f32[128,512]{1,0:T(8,128)}) custom-call(f32[4,512,512]{2,1,0:T(8,128)} %bitcast.8, f32[2,4,32,512]{3,2,1,0:T(8,128)} %bitcast.10, f32[4,32,512]{2,1,0:T(8,128)} %bitcast.12, s32[16]{0:T(128)} %tiles.1, s32[1,16,16]{2,1,0:T(8,128)} %mask.1, f32[1,2,16,16]{3,2,1,0:T(8,128)} %coef.1, f32[1,16]{1,0:T(1,128)} %center.1), custom_call_target="tpu_custom_call" | custom-call | tf_op jit(solution)/shard_map/window/pallas_call | solution.py:464
  182.6 0.0 copy-start
  182.6 3.9 %settle.1 = f32[4,512,512]{2,1,0:T(8,128)} custom-call(f32[4,512,512]{2,1,0:T(8,128)} %get-tuple-element.4.src), custom_call_target="tpu_custom_call" | custom-call | tf_op jit(solution)/shard_map/settle/pallas_call | solution.py:503
  186.5 0.0 copy-done
  186.5 0.7 copy.11
Async XLA Ops:
  182.6 3.9 %copy-start = (f32[128,512]{1,0:T(8,128)S(1)}, f32[128,512]{1,0:T(8,128)}, u32[]{:S(2)}) copy-start(f32[128,512]{1,0:T(8,128)} %get-tuple-element.5) | copy-start | bytes 786436

commit v4 on v3

--- a/solution.py
+++ b/solution.py
@@ -32,7 +32,7 @@
 
 
 def kernel(nsector, env, site, psi, tiles, mask, coef, center, fresh, hpsi,
-           own, rcv, f0, f1s, f1r, up, pack, got, fu, back0, back1, hbuf, z, zp, abuf, pbuf, q, s1, s2, table, place,
+           own, rcv, f0, f1s, f1r, up, pack, got, fu, back0, back1, hbuf, z, zp, abuf, pbuf, stage, total, q, s1, s2, table, place,
            load_sem, up_sem, shift_sem, own_send, own_recv, fwd_send, fwd_recv, f1_send, f1_recv,
            sh_send, sh_recv, bk_send, bk_recv, zp_send, zp_recv, out_sem, rs_send, rs_recv):
     section = lax.axis_index("section")
@@ -57,9 +57,7 @@
         lax.fori_loop(lo, hi, lambda i, c: (body(i), c)[1], 0)
 
     def load(k):
-        if k == A0:
-            src = site.at[0]
-        elif k == PSI:
+        if k == PSI:
             src = psi
         else:
             src = env.at[:, pl.ds(LOW.index(k) * CH, CH), :]
@@ -71,7 +69,7 @@
 
     load(0).start()
     loop(0, nsector, lambda u: load_up(u).start())
-    for k in LOW[1:] + (A0, PSI):
+    for k in LOW[1:] + (PSI,):
         load(k).start()
 
     barrier = pltpu.get_barrier_semaphore()
@@ -81,7 +79,7 @@
     pl.semaphore_wait(barrier, nsector + 2)
 
     def shift():
-        return remote(site.at[1], own.at[A1], shift_sem.at[0], shift_sem.at[1], above)
+        return remote(stage, own.at[A1], shift_sem.at[0], shift_sem.at[1], above)
 
     def rows_of(k):
         return pl.ds(0, CH)
@@ -105,7 +103,7 @@
                       fwd_send.at[1, k], fwd_recv.at[1, k], left)
 
     def issue(k):
-        if k in LOW + (A0, PSI):
+        if k in LOW + (PSI,):
             load(k).wait()
         to_right(k).start()
         to_left(k).start()
@@ -145,9 +143,10 @@
 
     for d in ORDER:
         send_share(d)
-    shift().start()
     issue(1)
     issue(2)
+    own[A0] = site[:, 0, :].reshape(4, CH, 512)
+    stage[...] = site[:, 1, :].reshape(4, CH, 512)
 
     for s in range(2):
         for d in range(4):
@@ -206,7 +205,7 @@
 
         loop(0, nrows // 8, rows)
 
-    def mix_low(e):
+    def mix_low(e, send=True):
         def put(r, acc):
             span = pl.ds(pl.multiple_of(r * 8, 8), 8)
             for v in range(4):
@@ -214,7 +213,8 @@
                 f1s[e, v, span, :] = acc[4 + v]
 
         mix(LOW[e], CH, put)
-        f1(e).start()
+        if send:
+            f1(e).start()
 
     def mix_shared(n):
         def put(r, acc):
@@ -294,9 +294,9 @@
 
     relay(0)
     relay(1)
-    mix_low(0)
+    mix_low(0, send=False)
     relay(2)
-    mix_low(1)
+    mix_low(1, send=False)
     loop(1, nsector, lambda d: share(d).wait_recv())
     for n in range(4):
         for i in range(4):
@@ -305,6 +305,9 @@
     issue(3)
     issue(4)
     issue(5)
+    f1(0).start()
+    f1(1).start()
+    shift().start()
     mix_low(2)
     relay(3)
     issue(6)
@@ -375,48 +378,54 @@
         exchange(v).wait_recv()
         lh, ll = halves(jnp.where(section == 0, z[v], zp[v]))
         x = dot3(lh, ll, pbuf[0], pbuf[1]) * center[0, y * 4 + v]
-        for h, part in enumerate(halves(x)):
-            hbuf[0, 0, h, v] = part[:256]
-            hbuf[0, 1, h, v] = part[256:]
-        rh, rl = halves(jnp.where(section == 0, zp[v], z[v]))
-        abuf[2 * v] = rh
-        abuf[2 * v + 1] = rl
-
-    loop(0, 4, apply_left)
-
-    def partial(b):
+        return halves(x), halves(jnp.where(section == 0, zp[v], z[v]))
+
+    total[...] = jnp.zeros_like(total)
+
+    def add(v):
+        (xh, xl), (rh, rl) = apply_left(v)
+        total[...] += dot3(xh, xl, rh, rl)
+
+    loop(0, 3, add)
+    for h, (x, r) in enumerate(zip(*apply_left(3))):
+        hbuf[0, 0, h, 0] = x[:256]
+        hbuf[0, 1, h, 0] = x[256:]
+        abuf[h] = r
+
+    def partial(slot, b):
         rows = pl.ds(pl.multiple_of((b % 2) * 128, 128), 128)
-        r = None
-        for v in range(4):
-            t = dot3(hbuf[0, b // 2, 0, v, rows, :], hbuf[0, b // 2, 1, v, rows, :], abuf[2 * v], abuf[2 * v + 1])
-            r = t if r is None else r + t
-        return r
-
-    hops = [
-        remote(q.at[0, 0], s1.at[0], rs_send.at[0], rs_recv.at[0], right),
-        remote(q.at[0, 1], s1.at[1], rs_send.at[1], rs_recv.at[1], left),
-        remote(q.at[1], s2.at[0], rs_send.at[2], rs_recv.at[2], right),
-        remote(q.at[2], s2.at[1], rs_send.at[3], rs_recv.at[3], left),
-    ]
-
-    def keep(slot, r):
+        r = dot3(hbuf[0, b // 2, 0, 0, rows, :], hbuf[0, b // 2, 1, 0, rows, :], abuf[0], abuf[1])
+        r += total[pl.ds(pl.multiple_of(b * 128, 128), 128), :]
         q[slot, 0] = r[:, :256]
         q[slot, 1] = r[:, 256:]
 
-    keep(0, partial((y + 2) % 4))
+    hops = [
+        remote(src, dst, rs_send.at[i], rs_recv.at[i], to) for i, (src, dst, to) in enumerate((
+            (q.at[0, 0], s1.at[0], right),
+            (q.at[0, 1], s1.at[1], left),
+            (q.at[1, 1], s2.at[0, 1], right),
+            (q.at[2, 0], s2.at[1, 0], left),
+            (q.at[1, 0], s2.at[0, 0], right),
+            (q.at[2, 1], s2.at[1, 1], left),
+        ))
+    ]
+
+    partial(0, (y + 2) % 4)
     hops[0].start()
     hops[1].start()
-    keep(1, partial((y + 1) % 4))
+    partial(1, (y + 1) % 4)
+    hops[2].start()
+    partial(2, (y + 3) % 4)
+    hops[3].start()
     hops[0].wait_recv()
     q[1, 0] += s1[0]
-    hops[2].start()
-    keep(2, partial((y + 3) % 4))
+    hops[4].start()
     hops[1].wait_recv()
     q[2, 1] += s1[1]
-    hops[3].start()
-    keep(3, partial(y))
-    hops[2].wait_recv()
-    hops[3].wait_recv()
+    hops[5].start()
+    partial(3, y)
+    for i in range(2, 6):
+        hops[i].wait_recv()
     for t in range(2):
         hpsi[:, pl.ds(t * 256, 256)] = q[3, t] + (s2[0, t] + s2[1, t])
 
@@ -457,7 +466,6 @@
 
 
 def local(env, site, sector_tiles, mpo_mask, mpo_coef, psi, center_coef):
-    spins = site[0].transpose(1, 0, 2).reshape(2, 4, CH, 512)
     anywhere = pl.BlockSpec(memory_space=pl.ANY)
     scalars = pl.BlockSpec(memory_space=pltpu.SMEM)
     dma = pltpu.SemaphoreType.DMA
@@ -467,7 +475,7 @@
             jax.ShapeDtypeStruct((4, 512, 512), F32),
             jax.ShapeDtypeStruct((128, 512), F32),
         ),
-        in_specs=[anywhere, anywhere, anywhere, scalars, scalars, scalars, scalars],
+        in_specs=[anywhere, pl.BlockSpec(memory_space=pltpu.VMEM), anywhere, scalars, scalars, scalars, scalars],
         out_specs=(anywhere, pl.BlockSpec(memory_space=pltpu.VMEM)),
         scratch_shapes=[
             pltpu.VMEM((NK, 4, CH, 512), F32),
@@ -486,6 +494,8 @@
             pltpu.VMEM((4, 512, 512), F32),
             pltpu.VMEM((8, 512, 512), BF16),
             pltpu.VMEM((2, 512, 512), BF16),
+            pltpu.VMEM((4, CH, 512), F32),
+            pltpu.VMEM((512, 512), F32),
             pltpu.VMEM((4, 2, 128, 256), F32),
             pltpu.VMEM((2, 128, 256), F32),
             pltpu.VMEM((2, 2, 128, 256), F32),
@@ -493,13 +503,13 @@
             pltpu.SMEM((48,), jnp.int32),
             dma((NK,)), dma((16,)), dma((2,)), dma((2, NK)), dma((2, NK)), dma((2, NK)), dma((2, NK)),
             dma((NL,)), dma((NL,)), dma((16,)), dma((16,)), dma((2, 2, 16)), dma((2, 2, 16)),
-            dma((4,)), dma((4,)), dma((4,)), dma((4,)), dma((4,)),
+            dma((4,)), dma((4,)), dma((4,)), dma((6,)), dma((6,)),
         ],
         compiler_params=pltpu.CompilerParams(
             collective_id=0, has_side_effects=True, vmem_limit_bytes=62 << 20
         ),
         name="window",
-    )(env[0], spins, psi[0].reshape(4, CH, 512), sector_tiles, mpo_mask, mpo_coef, center_coef)
+    )(env[0], site[0], psi[0].reshape(4, CH, 512), sector_tiles, mpo_mask, mpo_coef, center_coef)
     fresh = pl.pallas_call(
         settle,
         out_shape=jax.ShapeDtypeStruct((4, 512, 512), F32),

time: 190 us -> 186 us (0.979)
  Pallas kernels: 184 us -> 182 us
  local copies, waits for them, and re-layouts: 2.65 us -> 0.71 us
    pallas_call x1, Pallas kernels: 180 us -> 178 us  [local(): pl.pallas_call(functools.partial(kernel, sector_tiles.shape[0]), out_shap...]
    transpose x1 -> x0, local copies, waits for them, and re-layouts: 1.94 us -> none  [local(): spins = site[0].transpose(1, 0, 2).reshape(2, 4, CH, 512)]
where the time goes in v4:
time: 186 us; the launch traced here: 183 us
  Pallas kernels  182 us (98%)
    pallas_call x1, Pallas kernels, local(): pl.pallas_call(functools.partial(kernel, sector_tiles.shape[0]), out_shap...  178 us
    pallas_call x1, Pallas kernels, local(): pl.pallas_call(settle, out_shape=jax.ShapeDtypeStruct((4, 512, 512), F32)...  3.89 us

profile of v4, /device:TPU:6, one launch (start us, length us, event | category | flops | bytes accessed | tf_op | source)
XLA Modules:
  0.0 183.0 jit_solution(14441039807786138264)
XLA Ops:
  0.6 177.7 %window.1 = (f32[4,512,512]{2,1,0:T(8,128)}, f32[128,512]{1,0:T(8,128)}) custom-call(f32[4,512,512]{2,1,0:T(8,128)} %bitcast.5, f32[128,2,512]{2,1,0:T(2,128)} %bitcast.7, f32[4,32,512]{2,1,0:T(8,128)} %bitcast.8, s32[16]{0:T(128)} %tiles.1, s32[1,16,16]{2,1,0:T(8,128)} %mask.1, f32[1,2,16,16]{3,2,1,0:T(8,128)} %coef.1, f32[1,16]{1,0:T(1,128)} %center.1), custom_call_target="tpu_custom_call" | custom-call | tf_op jit(solution)/shard_map/window/pallas_call | solution.py:472
  178.4 0.0 copy-start
  178.4 3.9 %settle.1 = f32[4,512,512]{2,1,0:T(8,128)} custom-call(f32[4,512,512]{2,1,0:T(8,128)} %get-tuple-element.4.src), custom_call_target="tpu_custom_call" | custom-call | tf_op jit(solution)/shard_map/settle/pallas_call | solution.py:513
  182.3 0.0 copy-done
  182.3 0.7 copy.10
Async XLA Ops:
  178.4 3.9 %copy-start = (f32[128,512]{1,0:T(8,128)S(1)}, f32[128,512]{1,0:T(8,128)}, u32[]{:S(2)}) copy-start(f32[128,512]{1,0:T(8,128)} %get-tuple-element.5) | copy-start | bytes 786436

commit v5 on v4

--- a/solution.py
+++ b/solution.py
@@ -287,7 +287,7 @@
         for s in range(2):
             t = dot3(abuf[4 + s * 2, :, cols], abuf[5 + s * 2, :, cols], hbuf[group, s, 0, v], hbuf[group, s, 1, v])
             r = t if r is None else r + t
-        if group == 0:
+        if group == 1:
             z[v] = r
         else:
             z[v] += r
@@ -343,23 +343,24 @@
     mix_low(5)
     relay(13)
     mix_low(6)
-    given(0)
-    first_shared(0)
     relay(14)
     mix_low(7)
     first_low(0, 1)
+    given(0)
+    first_shared(0)
     arrived(PSI)
     for d in range(4):
         row0 = pl.multiple_of(((y + d) % 4) * 128, 128)
         for h, part in enumerate(halves(piece(d, PSI).reshape(128, 512))):
             pbuf[h, pl.ds(row0, 128), :] = part
 
-    for g in range(2):
-        loop(4 * g, 4 * g + 4, lambda e: f1(e).wait_recv())
-        first_low(1, g)
-    loop(0, 4, lambda v: second(0, v))
+    loop(0, 4, lambda e: f1(e).wait_recv())
+    first_low(1, 0)
     given(1)
     first_shared(1)
+    loop(0, 4, lambda v: second(1, v))
+    loop(4, 8, lambda e: f1(e).wait_recv())
+    first_low(1, 1)
 
     def exchange(v):
         return remote(z.at[v], zp.at[v], zp_send.at[v], zp_recv.at[v], other)
@@ -368,7 +369,7 @@
         return pltpu.make_async_copy(z.at[v], fresh.at[v], out_sem.at[v])
 
     def finish(v):
-        second(1, v)
+        second(0, v)
         exchange(v).start()
         out(v).start()
 

time: 186 us -> 182 us (0.978)
  Pallas kernels: 182 us -> 179 us
    pallas_call x1, Pallas kernels: 178 us -> 175 us  [local(): pl.pallas_call(functools.partial(kernel, sector_tiles.shape[0]), out_shap...]
where the time goes in v5:
time: 182 us; the launch traced here: 180 us
  Pallas kernels  179 us (98%)
    pallas_call x1, Pallas kernels, local(): pl.pallas_call(functools.partial(kernel, sector_tiles.shape[0]), out_shap...  175 us
    pallas_call x1, Pallas kernels, local(): pl.pallas_call(settle, out_shape=jax.ShapeDtypeStruct((4, 512, 512), F32)...  3.89 us

profile of v5, /device:TPU:6, one launch (start us, length us, event | category | flops | bytes accessed | tf_op | source)
XLA Modules:
  0.0 180.4 jit_solution(15935262002820493373)
XLA Ops:
  0.6 175.1 %window.1 = (f32[4,512,512]{2,1,0:T(8,128)}, f32[128,512]{1,0:T(8,128)}) custom-call(f32[4,512,512]{2,1,0:T(8,128)} %bitcast.5, f32[128,2,512]{2,1,0:T(2,128)} %bitcast.7, f32[4,32,512]{2,1,0:T(8,128)} %bitcast.8, s32[16]{0:T(128)} %tiles.1, s32[1,16,16]{2,1,0:T(8,128)} %mask.1, f32[1,2,16,16]{3,2,1,0:T(8,128)} %coef.1, f32[1,16]{1,0:T(1,128)} %center.1), custom_call_target="tpu_custom_call" | custom-call | tf_op jit(solution)/shard_map/window/pallas_call | solution.py:473
  175.8 0.0 copy-start
  175.8 3.9 %settle.1 = f32[4,512,512]{2,1,0:T(8,128)} custom-call(f32[4,512,512]{2,1,0:T(8,128)} %get-tuple-element.4.src), custom_call_target="tpu_custom_call" | custom-call | tf_op jit(solution)/shard_map/settle/pallas_call | solution.py:514
  179.7 0.0 copy-done
  179.7 0.7 copy.10
Async XLA Ops:
  175.8 3.9 %copy-start = (f32[128,512]{1,0:T(8,128)S(1)}, f32[128,512]{1,0:T(8,128)}, u32[]{:S(2)}) copy-start(f32[128,512]{1,0:T(8,128)} %get-tuple-element.5) | copy-start | bytes 786436

commit v6 on v5

--- a/solution.py
+++ b/solution.py
@@ -262,14 +262,14 @@
                 for v in range(4):
                     hbuf[group, s, h, v, pl.ds(pl.multiple_of(at + u * rows, 16), rows), :] = part[u, v]
 
-    def first_low(s, g):
+    def first_low(s, g, lo=0, hi=2):
         def half(t):
             at = 4 * g + 2 * t
             lhs = (f0 if s == 0 else f1r)[pl.ds(at, 2)]
             ah, al = halves(lhs.reshape(256, 512))
             store_h(0, s, dot3(ah, al, abuf[s * 2], abuf[s * 2 + 1]), 2, CH, at * CH)
 
-        loop(0, 2, half)
+        loop(lo, hi, half)
 
     def first_shared(s):
         home = sector if s == 0 else before
@@ -281,10 +281,10 @@
 
         loop(0, 4, quarter)
 
-    def second(group, v):
+    def second(group, v, spins=(0, 1)):
         cols = pl.ds(group * 256, 256)
         r = None
-        for s in range(2):
+        for s in spins:
             t = dot3(abuf[4 + s * 2, :, cols], abuf[5 + s * 2, :, cols], hbuf[group, s, 0, v], hbuf[group, s, 1, v])
             r = t if r is None else r + t
         if group == 1:
@@ -359,8 +359,10 @@
     given(1)
     first_shared(1)
     loop(0, 4, lambda v: second(1, v))
-    loop(4, 8, lambda e: f1(e).wait_recv())
-    first_low(1, 1)
+    loop(0, 4, lambda v: second(0, v, (0,)))
+    for t in range(2):
+        loop(4 + 2 * t, 6 + 2 * t, lambda e: f1(e).wait_recv())
+        first_low(1, 1, t, t + 1)
 
     def exchange(v):
         return remote(z.at[v], zp.at[v], zp_send.at[v], zp_recv.at[v], other)
@@ -369,7 +371,7 @@
         return pltpu.make_async_copy(z.at[v], fresh.at[v], out_sem.at[v])
 
     def finish(v):
-        second(0, v)
+        second(0, v, (1,))
         exchange(v).start()
         out(v).start()
 

time: 182 us -> 185 us (1.016)
  Pallas kernels: 179 us -> 181 us
where the time goes in v6:
time: 185 us; the launch traced here: 182 us
  Pallas kernels  181 us (98%)
    pallas_call x1, Pallas kernels, local(): pl.pallas_call(functools.partial(kernel, sector_tiles.shape[0]), out_shap...  177 us
    pallas_call x1, Pallas kernels, local(): pl.pallas_call(settle, out_shape=jax.ShapeDtypeStruct((4, 512, 512), F32)...  3.89 us

profile of v6, /device:TPU:6, one launch (start us, length us, event | category | flops | bytes accessed | tf_op | source)
XLA Modules:
  0.0 181.9 jit_solution(13582504647433024297)
XLA Ops:
  0.6 176.6 %window.1 = (f32[4,512,512]{2,1,0:T(8,128)}, f32[128,512]{1,0:T(8,128)}) custom-call(f32[4,512,512]{2,1,0:T(8,128)} %bitcast.5, f32[128,2,512]{2,1,0:T(2,128)} %bitcast.7, f32[4,32,512]{2,1,0:T(8,128)} %bitcast.8, s32[16]{0:T(128)} %tiles.1, s32[1,16,16]{2,1,0:T(8,128)} %mask.1, f32[1,2,16,16]{3,2,1,0:T(8,128)} %coef.1, f32[1,16]{1,0:T(1,128)} %center.1), custom_call_target="tpu_custom_call" | custom-call | tf_op jit(solution)/shard_map/window/pallas_call | solution.py:475
  177.3 0.0 copy-start
  177.3 3.9 %settle.1 = f32[4,512,512]{2,1,0:T(8,128)} custom-call(f32[4,512,512]{2,1,0:T(8,128)} %get-tuple-element.4.src), custom_call_target="tpu_custom_call" | custom-call | tf_op jit(solution)/shard_map/settle/pallas_call | solution.py:516
  181.2 0.0 copy-done
  181.2 0.7 copy.10
Async XLA Ops:
  177.3 3.9 %copy-start = (f32[128,512]{1,0:T(8,128)S(1)}, f32[128,512]{1,0:T(8,128)}, u32[]{:S(2)}) copy-start(f32[128,512]{1,0:T(8,128)} %get-tuple-element.5) | copy-start | bytes 786436
